TPU v7x, 256 devices: a whole 4x4x8 slice. The times are simulated.
256 devices in a mesh: keys: 64 (over y, z, core), seq: 4 (over x).
Axes of the slice: x: 4, y: 4, z: 8, core: 2. Of those that a mesh axis runs over, the one named last changes fastest.
Arguments:
- span_queries: bfloat16 [1536, 768], P(('keys', 'seq')), may hold values from -6 to 6
- key_slab: bfloat16 [4096, 768], P('keys'), may hold values from -0.21875 to 0.21875
- neighbour_store: bfloat16 [4096, 64, 896], P('keys'), may hold values from -6 to 6
- neighbour_ids: int32 [1536, 2], P(('keys', 'seq')), may hold values from 0 to 4094, as said below
- attn_queries: bfloat16 [98304, 2048], P(('keys', 'seq')), may hold values from -200 to 200
- kv_weight: bfloat16 [2, 2048, 896], P(None, 'keys'), may hold values from -0.1875 to 0.1875
Outputs:
- best_scores: float32 [1536, 2], P(('keys', 'seq'))
- attended: bfloat16 [98304, 2048], P(('keys', 'seq'))
Inputs may be any that keep to these rules, and one draw needn't show every extreme that they name: `neighbour_ids`: each id c has c mod 64 at most 62, so c + 1 lies on the same shard c // 64. Among the 12 ids of one device's spans (aligned blocks of 6 rows), no shard holds more than 1, and some shard holds exactly 1.
All inputs are finite; a program needn't handle non-finite values.
Results may differ from a plain program's by a relative error of at most 0.012.
The roundings to bfloat16 on the way count: a program that leaves them out, or rounds other values in their place, can miss the bound.
Values may be sent and summed in bfloat16 or wider, within the bound.
A program may use at most 128 MiB of HBM per device.

v0:
```python
import jax
import jax.numpy as jnp
from jax import lax
from jax.sharding import PartitionSpec as P

HEADS = 16
HEAD_DIM = 128


def merged(part, axis, combine):
    gathered = jax.tree.map(lambda a: lax.all_gather(a, axis), part)

    def take(source):
        return jax.tree.map(lambda a: lax.dynamic_index_in_dim(a, source, 0, False), gathered)

    return lax.fori_loop(
        1, lax.axis_size(axis), lambda source, state: combine(state, take(source)), take(0)
    )


def keep_two(left, right):
    higher = jnp.maximum(left[0], right[0])
    runner = jnp.maximum(jnp.minimum(left[0], right[0]), jnp.maximum(left[1], right[1]))
    return (higher, runner)


def best_two(values):
    padding = jnp.full((values.shape[0], 2), -jnp.inf, values.dtype)
    return lax.top_k(jnp.concatenate([values, padding], axis=1), 2)[0]


def row_scores(left, right):
    return lax.dot_general(
        left, right, (((1,), (1,)), ((), ())), preferred_element_type=jnp.float32
    )


def body(span_queries, key_slab, neighbour_store, neighbour_ids, attn_queries, kv_weight):
    key_count = lax.axis_size("keys")
    position = lax.axis_index("keys")
    own_spans = neighbour_ids.shape[0]
    shard_spans = neighbour_store.shape[0]
    span_rows = neighbour_store.shape[1]
    enc_width = neighbour_store.shape[2]
    candidates = best_two(
        row_scores(lax.all_gather(span_queries, "keys", axis=0, tiled=True), key_slab)
    )
    higher_all, runner_all = merged((candidates[:, 0], candidates[:, 1]), "keys", keep_two)
    higher = lax.dynamic_slice_in_dim(higher_all, position * own_spans, own_spans)
    runner = lax.dynamic_slice_in_dim(runner_all, position * own_spans, own_spans)
    best_scores = jnp.stack([higher, runner], axis=1)
    flat_ids = neighbour_ids.reshape(-1)
    need_count = flat_ids.shape[0]
    per_shard = (need_count + key_count - 1) // key_count
    capacity = 2 * per_shard
    target = flat_ids // shard_spans
    offset = flat_ids % shard_spans
    order_index = jnp.arange(need_count, dtype=jnp.int32)
    same_shard = (target[:, None] == target[None, :]) & (
        order_index[:, None] < order_index[None, :]
    )
    slot_base = 2 * jnp.sum(same_shard.astype(jnp.int32), axis=0)
    slot_index = jnp.arange(capacity, dtype=jnp.int32)
    shard_onehot = (target[:, None] == jnp.arange(key_count, dtype=jnp.int32)[None, :]).astype(
        jnp.int32
    )
    first_slot = (slot_index == slot_base[..., None]).astype(jnp.int32) * offset[..., None]
    next_slot = (slot_index == slot_base[..., None] + 1).astype(jnp.int32) * (offset[..., None] + 1)
    table = jnp.einsum("nj,ns->js", shard_onehot, first_slot + next_slot)
    incoming = lax.all_to_all(table, "keys", split_axis=0, concat_axis=0, tiled=True)
    outgoing = neighbour_store[incoming]
    arrived = lax.all_to_all(outgoing, "keys", split_axis=0, concat_axis=0, tiled=True)
    arrived = arrived.reshape(key_count * capacity, span_rows, enc_width)
    first_row = target * capacity + slot_base
    picked = arrived[jnp.stack([first_row, first_row + 1], axis=1)]
    neighbours = picked.reshape(own_spans * 4 * span_rows, enc_width)
    keys_values = jnp.einsum(
        "re,tce->rtc",
        neighbours,
        lax.all_gather(kv_weight, "keys", axis=1, tiled=True),
        preferred_element_type=jnp.float32,
    ).astype(jnp.bfloat16)
    key_rows = keys_values[:, 0].reshape(own_spans, 4 * span_rows, HEADS, HEAD_DIM)
    value_rows = keys_values[:, 1].reshape(own_spans, 4 * span_rows, HEADS, HEAD_DIM)
    queries = attn_queries.reshape(own_spans, span_rows, HEADS, HEAD_DIM)
    logits = jnp.einsum(
        "cqhd,ckhd->chqk", queries, key_rows, preferred_element_type=jnp.float32
    ) * HEAD_DIM ** (-0.5)
    largest = jnp.max(logits, axis=-1, keepdims=True)
    expo_terms = jnp.exp(logits - largest)
    weights = (expo_terms / jnp.sum(expo_terms, axis=-1, keepdims=True)).astype(jnp.bfloat16)
    output = jnp.einsum("chqk,ckhd->cqhd", weights, value_rows, preferred_element_type=jnp.float32)
    attended = output.astype(jnp.bfloat16).reshape(own_spans * span_rows, HEADS * HEAD_DIM)
    return (best_scores, attended)


def solution(mesh):
    return jax.shard_map(
        body,
        mesh=mesh,
        in_specs=(
            P(("keys", "seq"), None),
            P("keys", None),
            P("keys", None, None),
            P(("keys", "seq"), None),
            P(("keys", "seq"), None),
            P(None, "keys", None),
        ),
        out_specs=(P(("keys", "seq"), None), P(("keys", "seq"), None)),
        check_vma=False,
    )
```

profile of v0, /device:TPU:1, one launch (start us, length us, event | category | flops | bytes accessed | tf_op | source)
XLA Modules:
  0.0 606.7 jit_solution(17030885371384447195)
XLA Ops:
  7.2 0.0 copy-start
  7.2 0.8 copy.33
  8.0 0.1 reshape.394
  8.1 0.1 convert_reduce_fusion
  8.2 0.3 fusion.23
  8.5 22.2 %all_to_all.17 = s32[64,1,2]{2,1,0:T(1,128)S(1)} all-to-all(s32[64,1,2]{2,1,0:T(1,128)S(1)} %bitcast.81), channel_id=1, replica_groups=mesh['keys'=64,'seq'=4] {'keys'}, dimensions={0} | all-to-all | bytes 1024 | tf_op jit(solution)/shard_map/all_to_all | solution.py:70
  30.7 0.1 copy.35
  30.8 0.1 copy.36
  30.9 0.1 reshape.402
  31.1 11.9 %gather_fusion = bf16[128,64,896]{2,1,0:T(8,128)(2,1)} fusion(bf16[64,64,896]{2,1,0:T(8,128)(2,1)} %param.10, s32[1024]{0:T(1024)S(1)} %pad_clamp_fusion.1), kind=kCustom, calls=%fused_computation | custom fusion | bytes 29360640 | tf_op jit(solution)/shard_map/gather | solution.py:71
  43.0 0.0 copy-start.3
  43.0 6.2 %all-to-all-start.1 = ((bf16[64,2,64,896]{3,2,1,0:T(8,128)(2,1)}), bf16[64,2,64,896]{3,2,1,0:T(8,128)(2,1)}, u32[]{:S(2)}, u32[]{:S(2)}) async-start(bf16[64,2,64,896]{3,2,1,0:T(8,128)(2,1)} %bitcast.73), calls=%async_computation.1 | async-start | bytes 29360128 | tf_op jit(solution)/shard_map/all_to_all | solution.py:72
  49.2 0.0 all-gather.5.cloned.1.call-start
  49.3 0.7 all-gather.5.cloned.1.call-update
  50.0 0.1 reshape.396
  50.1 0.1 copy.38
  50.2 0.1 reshape.410
  50.2 0.0 copy-done.3
  50.3 1.6 copy.44
  51.8 0.0 copy-done.4
  51.8 380.2 %all-gather.2 = bf16[64,6,768]{2,1,0:T(8,128)(2,1)S(1)} all-gather(bf16[1,6,768]{2,1,0:T(8,128)(2,1)S(1)} %bitcast.82), channel_id=1, replica_groups=mesh['keys'=64,'seq'=4] {'keys'}, dimensions={0}, use_global_device_ids=true | all-gather | bytes 599040 | tf_op jit(solution)/shard_map/all_gather | solution.py:46
  432.0 0.2 reshape.426
  432.2 0.0 copy-done
  432.2 0.3 fusion.43
  432.5 5.0 top_k.8
  437.6 48.6 %all-gather = f32[24576,1]{0,1:T(1,128)S(1)} all-gather(f32[384,1]{0,1:T(1,128)S(1)} %get-tuple-element.161), channel_id=2, replica_groups=mesh['keys'=64,'seq'=4] {'keys'}, dimensions={0}, use_global_device_ids=true | all-gather | bytes 99840 | tf_op jit(solution)/shard_map/all_gather | solution.py:11
  486.2 0.5 broadcast.499
  486.7 0.9 reduce.14
  487.6 44.4 %all-gather.1 = f32[24576,1]{0,1:T(1,128)S(1)} all-gather(f32[384,1]{0,1:T(1,128)S(1)} %get-tuple-element.160), channel_id=3, replica_groups=mesh['keys'=64,'seq'=4] {'keys'}, dimensions={0}, use_global_device_ids=true | all-gather | bytes 99840 | tf_op jit(solution)/shard_map/all_gather | solution.py:11
  532.0 0.9 reduce.15
  533.0 4.3 while.17
  537.3 0.1 dynamic-slice_bitcast_fusion
  537.4 0.6 pad_maximum_fusion
  538.0 0.0 all-to-all-done.1
  538.0 6.3 %gather_fusion.1 = bf16[24,64,896]{2,1,0:T(8,128)(2,1)S(1)} fusion(bf16[128,64,896]{2,1,0:T(8,128)(2,1)} %bitcast.6, s32[1024]{0:T(1024)S(1)} %pad_clamp_fusion), kind=kCustom, calls=%fused_computation.1 | custom fusion | bytes 5505120 | tf_op jit(solution)/shard_map/gather | solution.py:75
  544.2 0.0 all-gather.5.cloned.1.call-done
  544.3 18.7 %convolution_convert_fusion = bf16[1536,2,2048]{2,0,1:T(8,128)(2,1)} fusion(bf16[1536,896,1]{1,0,2:T(8,128)(2,1)S(1)} %bitcast.78, bf16[2,2048,896]{2,1,0:T(8,128)(2,1)} %all-gather.5.cloned.1.call-done), kind=kOutput, calls=%fused_computation.6 | convolution fusion | flops 11280580608 | bytes 22675456 | tf_op jit(solution)/shard_map/re,tce->rtc/dot_general | solution.py:77
  563.0 5.3 slice_bitcast_fusion.1
  568.3 2.3 copy.43
  570.7 3.7 fusion.5
  574.4 0.0 copy-start.2
  574.4 2.4 fusion.42
  576.8 5.0 copy.45
  581.8 0.0 copy-done.2
  581.8 15.5 %fusion.16 = bf16[6,64,16,128]{3,1,2,0:T(8,128)(2,1)S(1)} fusion(bf16[6,256,16,128]{3,2,1,0:T(8,128)(2,1)} %bitcast.75, f32[6,16,64]{2,1,0:T(8,128)S(1)} %fusion.42, f32[6,16,256,64]{2,3,1,0:T(8,128)} %copy-done.2), kind=kOutput, calls=%fused_computation.24 | convolution fusion | flops 411310336 | bytes 14180352 | tf_op jit(solution)/shard_map/chqk,ckhd->cqhd/dot_general | solution.py:92
  597.3 1.0 copy.42
  598.4 1.6 copy.58
  599.9 0.0 copy-done.1
  (142 shorter events, 2.7 us)
Async XLA Ops:
  7.2 425.0 %copy-start = (bf16[64,768]{1,0:T(8,128)(2,1)S(1)}, bf16[64,768]{1,0:T(8,128)(2,1)}, u32[]{:S(2)}) copy-start(bf16[64,768]{1,0:T(8,128)(2,1)} %param.9) | copy-start | bytes 294916
  43.0 7.3 %copy-start.3 = (bf16[384,2048]{1,0:T(8,128)(2,1)S(1)}, bf16[384,2048]{1,0:T(8,128)(2,1)}, u32[]{:S(2)}) copy-start(bf16[384,2048]{1,0:T(8,128)(2,1)} %param.12) | copy-start | bytes 4718596
  43.0 8.8 %copy-start.4 = (bf16[6,768]{1,0:T(8,128)(2,1)S(1)}, bf16[6,768]{1,0:T(8,128)(2,1)}, u32[]{:S(2)}) copy-start(bf16[6,768]{1,0:T(8,128)(2,1)} %param.8) | copy-start | bytes 27652
  43.0 495.0 %all-to-all-start.1 = ((bf16[64,2,64,896]{3,2,1,0:T(8,128)(2,1)}), bf16[64,2,64,896]{3,2,1,0:T(8,128)(2,1)}, u32[]{:S(2)}, u32[]{:S(2)}) async-start(bf16[64,2,64,896]{3,2,1,0:T(8,128)(2,1)} %bitcast.73), calls=%async_computation.1 | async-start | bytes 29360128 | tf_op jit(solution)/shard_map/all_to_all | solution.py:72
  49.2 495.1 %all-gather.5.cloned.1.call-start = ((), (), s32[]{:S(2)}) async-start(), calls=%async_computation.2 | async-start | bytes 7454720 | tf_op jit(solution)/shard_map/all_gather | solution.py:80
  574.4 7.4 %copy-start.2 = (f32[6,16,256,64]{2,3,1,0:T(8,128)}, f32[6,16,256,64]{2,3,1,0:T(8,128)S(1)}, u32[]{:S(2)}) copy-start(f32[6,16,256,64]{2,3,1,0:T(8,128)S(1)} %fusion.5) | copy-start | bytes 18874372
  581.8 18.1 %copy-start.1 = (bf16[64,768]{1,0:T(8,128)(2,1)S(1)}, bf16[64,768]{1,0:T(8,128)(2,1)}, u32[]{:S(2)}) copy-start(bf16[64,768]{1,0:T(8,128)(2,1)} %param.9) | copy-start | bytes 294916
Sparse Core Ops, SparseCore 0:
  52.8 128.8 all-gather.4
where the time goes:
time: 607 us
  blocking collectives  495 us (82%)
  local copies, waits for them, and re-layouts  39 us (6%)
  matrix products  38.6 us (6%)
  between operations  14.2 us (2%)
  other arithmetic  10.8 us (2%)
  starting transfers between devices  6.27 us (1%)
    all_gather x1, blocking collectives, body(): lax.all_gather(span_queries, 'keys', axis=0, tiled=True)  380 us
    all_gather x2, blocking collectives, merged(): gathered = jax.tree.map(lambda a: lax.all_gather(a, axis), part)  93 us
    all_to_all x1, blocking collectives, body(): lax.all_to_all(table, 'keys', split_axis=0, concat_axis=0, tiled=True)  22.2 us
    dot_general x1, matrix products, body(): jnp.einsum('re,tce->rtc', neighbours, lax.all_gather(kv_weight, 'keys', a...  18.7 us
    unnamed x17, local copies, waits for them, and re-layouts  16.8 us
    dot_general x1, matrix products, body(): jnp.einsum('chqk,ckhd->cqhd', weights, value_rows, preferred_element_type...  15.5 us
  transfers between devices with their start and end apart: 2, of which 0 were waited for; matrix products, arithmetic and copies ran while one was open for 3% of the time, Pallas kernels for 0%

commit v1 on v0

--- a/solution.py
+++ b/solution.py
@@ -5,6 +5,28 @@
 
 HEADS = 16
 HEAD_DIM = 128
+
+
+def measure_quarters(frame_in, axis_k):
+    raw_out = list(frame_in.shape[1:])
+    raw_out[axis_k] *= frame_in.shape[0]
+    oldest = jnp.moveaxis(frame_in, 0, axis_k).reshape(raw_out)
+    return oldest
+
+
+def orders_unite(x0, group_axis):
+    q_n = jax.lax.axis_size(group_axis)
+    vec_out = x0[None]
+    for kk in range(q_n.bit_length() - 1):
+        aux = 1 << kk
+        store = []
+        for to_i in tuple(range(q_n)):
+            store.append((to_i, to_i ^ aux))
+        x_new = jax.lax.ppermute(vec_out, axis_name=group_axis, perm=store)
+        part_next = jnp.stack([vec_out, x_new], 0)
+        local_now = jax.lax.axis_index(group_axis) >> kk & 1
+        vec_out = jnp.where(local_now == 0, part_next, part_next[::-1]).reshape(-1, *x0.shape)
+    return vec_out
 
 
 def merged(part, axis, combine):
@@ -36,15 +58,18 @@
 
 
 def body(span_queries, key_slab, neighbour_store, neighbour_ids, attn_queries, kv_weight):
+
+    def _attach_types(vals, local_values, ndim_at):
+        last = measure_quarters(orders_unite(vals, local_values), ndim_at)
+        return last
+
     key_count = lax.axis_size("keys")
     position = lax.axis_index("keys")
     own_spans = neighbour_ids.shape[0]
     shard_spans = neighbour_store.shape[0]
     span_rows = neighbour_store.shape[1]
     enc_width = neighbour_store.shape[2]
-    candidates = best_two(
-        row_scores(lax.all_gather(span_queries, "keys", axis=0, tiled=True), key_slab)
-    )
+    candidates = best_two(row_scores(_attach_types(span_queries, "keys", 0), key_slab))
     higher_all, runner_all = merged((candidates[:, 0], candidates[:, 1]), "keys", keep_two)
     higher = lax.dynamic_slice_in_dim(higher_all, position * own_spans, own_spans)
     runner = lax.dynamic_slice_in_dim(runner_all, position * own_spans, own_spans)

time: 607 us -> 577 us (0.951)
  blocking collectives: 495 us -> 117 us
  waiting for transfers between devices: 0.7 us -> 336 us
  starting transfers between devices: 6.27 us -> 18.8 us
    all_gather x1 -> x0, blocking collectives: 380 us -> none  [body(): lax.all_gather(span_queries, 'keys', axis=0, tiled=True)]
    ppermute x0 -> x6, waiting for transfers between devices: none -> 336 us  [orders_unite(): x_new = jax.lax.ppermute(vec_out, axis_name=group_axis, perm=store)]
    ppermute x0 -> x6, starting transfers between devices: none -> 12.5 us  [orders_unite(): x_new = jax.lax.ppermute(vec_out, axis_name=group_axis, perm=store)]
    unnamed x17 -> x16, local copies, waits for them, and re-layouts: 16.8 us -> 16.6 us
  transfers between devices with their start and end apart: 2 -> 8, of which waited for: 0 -> 6; matrix products, arithmetic and copies ran while one was open for 3% -> 3% of each run, Pallas kernels for 0% -> 0%
where the time goes in v1:
time: 577 us
  waiting for transfers between devices  336 us (58%)
  blocking collectives  117 us (20%)
  local copies, waits for them, and re-layouts  39 us (7%)
  matrix products  38.6 us (7%)
  starting transfers between devices  18.8 us (3%)
  between operations  14.3 us (2%)
  other arithmetic  11.4 us (2%)
    ppermute x6, waiting for transfers between devices, orders_unite(): x_new = jax.lax.ppermute(vec_out, axis_name=group_axis, perm=store)  336 us
    all_gather x2, blocking collectives, merged(): gathered = jax.tree.map(lambda a: lax.all_gather(a, axis), part)  95.1 us
    all_to_all x1, blocking collectives, body(): lax.all_to_all(table, 'keys', split_axis=0, concat_axis=0, tiled=True)  22.2 us
    dot_general x1, matrix products, body(): jnp.einsum('re,tce->rtc', neighbours, lax.all_gather(kv_weight, 'keys', a...  18.7 us
    unnamed x16, local copies, waits for them, and re-layouts  16.6 us
    dot_general x1, matrix products, body(): jnp.einsum('chqk,ckhd->cqhd', weights, value_rows, preferred_element_type...  15.5 us
    ppermute x6, starting transfers between devices, orders_unite(): x_new = jax.lax.ppermute(vec_out, axis_name=group_axis, perm=store)  12.5 us
    gather x1, local copies, waits for them, and re-layouts, body(): outgoing = neighbour_store[incoming]  11.9 us
  transfers between devices with their start and end apart: 8, of which 6 were waited for; matrix products, arithmetic and copies ran while one was open for 3% of the time, Pallas kernels for 0%

profile of v1, /device:TPU:1, one launch (start us, length us, event | category | flops | bytes accessed | tf_op | source)
XLA Modules:
  0.0 577.0 jit_solution(10456691162956033047)
XLA Ops:
  7.2 0.8 copy.33
  8.0 0.1 reshape.414
  8.1 0.1 convert_reduce_fusion
  8.2 0.3 fusion.25
  8.5 22.2 %all_to_all.17 = s32[64,1,2]{2,1,0:T(1,128)S(1)} all-to-all(s32[64,1,2]{2,1,0:T(1,128)S(1)} %bitcast.112), channel_id=1, replica_groups=mesh['keys'=64,'seq'=4] {'keys'}, dimensions={0} | all-to-all | bytes 1024 | tf_op jit(solution)/shard_map/all_to_all | solution.py:95
  30.8 0.1 copy.36
  30.9 0.1 reshape.422
  31.1 11.9 %gather_fusion = bf16[128,64,896]{2,1,0:T(8,128)(2,1)} fusion(bf16[64,64,896]{2,1,0:T(8,128)(2,1)} %param.10, s32[1024]{0:T(1024)S(1)} %pad_clamp_fusion.1), kind=kCustom, calls=%fused_computation | custom fusion | bytes 29360640 | tf_op jit(solution)/shard_map/gather | solution.py:96
  43.0 6.2 %all-to-all-start.1 = ((bf16[64,2,64,896]{3,2,1,0:T(8,128)(2,1)}), bf16[64,2,64,896]{3,2,1,0:T(8,128)(2,1)}, u32[]{:S(2)}, u32[]{:S(2)}) async-start(bf16[64,2,64,896]{3,2,1,0:T(8,128)(2,1)} %bitcast.92), calls=%async_computation.1 | async-start | bytes 29360128 | tf_op jit(solution)/shard_map/all_to_all | solution.py:97
  49.3 0.7 collective-permute-start
  50.0 0.8 collective-permute-done
  50.9 1.2 collective-permute-start.1
  52.1 315.1 %collective-permute-done.1 = bf16[2,6,768]{2,1,0:T(8,128)(2,1)S(1)} collective-permute-done((bf16[2,6,768]{2,1,0:T(8,128)(2,1)S(1)}, bf16[2,6,768]{2,1,0:T(8,128)(2,1)S(1)}, u32[]{:S(2)}, u32[]{:S(2)}) %collective-permute-start.1) | collective-permute-done | bytes 18464 | tf_op jit(solution)/shard_map/ppermute | solution.py:25
  367.2 0.1 collective-permute-start.2
  367.3 4.3 collective-permute-done.2
  371.7 4.3 collective-permute-start.3
  376.0 4.6 collective-permute-done.3
  380.6 3.6 collective-permute-start.4
  384.3 4.4 collective-permute-done.4
  388.7 0.1 pad_maximum_fusion.1
  388.9 2.6 collective-permute-start.5
  391.5 0.1 copy.38
  391.6 0.1 reshape.430
  391.7 1.6 copy.44
  393.3 6.6 %collective-permute-done.5 = bf16[32,6,768]{2,1,0:T(8,128)(2,1)S(1)} collective-permute-done((bf16[32,6,768]{2,1,0:T(8,128)(2,1)S(1)}, bf16[32,6,768]{2,1,0:T(8,128)(2,1)S(1)}, u32[]{:S(2)}, u32[]{:S(2)}) %collective-permute-start.5) | collective-permute-done | bytes 294944 | tf_op jit(solution)/shard_map/ppermute | solution.py:25
  399.9 0.2 pad_maximum_fusion
  400.1 0.1 reverse_select_fusion
  400.2 0.2 reshape_reshape.3
  400.4 0.3 fusion.45
  400.8 5.0 top_k.8
  405.8 49.6 %all-gather = f32[24576,1]{0,1:T(1,128)S(1)} all-gather(f32[384,1]{0,1:T(1,128)S(1)} %get-tuple-element.161), channel_id=2, replica_groups=mesh['keys'=64,'seq'=4] {'keys'}, dimensions={0}, use_global_device_ids=true | all-gather | bytes 99840 | tf_op jit(solution)/shard_map/all_gather | solution.py:33
  455.4 45.5 %all-gather.1 = f32[24576,1]{0,1:T(1,128)S(1)} all-gather(f32[384,1]{0,1:T(1,128)S(1)} %get-tuple-element.160), channel_id=3, replica_groups=mesh['keys'=64,'seq'=4] {'keys'}, dimensions={0}, use_global_device_ids=true | all-gather | bytes 99840 | tf_op jit(solution)/shard_map/all_gather | solution.py:33
  500.9 0.5 broadcast.499
  501.5 0.9 reduce.14
  502.4 0.9 reduce.15
  503.3 4.3 while.17
  507.6 0.1 dynamic-slice_bitcast_fusion
  507.7 0.6 pad_maximum_fusion.6
  508.3 6.3 %gather_fusion.1 = bf16[24,64,896]{2,1,0:T(8,128)(2,1)S(1)} fusion(bf16[128,64,896]{2,1,0:T(8,128)(2,1)} %bitcast.23, s32[1024]{0:T(1024)S(1)} %pad_clamp_fusion), kind=kCustom, calls=%fused_computation.1 | custom fusion | bytes 5505120 | tf_op jit(solution)/shard_map/gather | solution.py:100
  514.6 18.7 %convolution_convert_fusion = bf16[1536,2,2048]{2,0,1:T(8,128)(2,1)} fusion(bf16[1536,896,1]{1,0,2:T(8,128)(2,1)S(1)} %bitcast.97, bf16[2,2048,896]{2,1,0:T(8,128)(2,1)} %all-gather.4.cloned.1.call-done), kind=kOutput, calls=%fused_computation.6 | convolution fusion | flops 11280580608 | bytes 22675456 | tf_op jit(solution)/shard_map/re,tce->rtc/dot_general | solution.py:102
  533.3 5.3 slice_bitcast_fusion.1
  538.6 2.3 copy.43
  541.0 3.7 fusion.5
  544.7 2.4 fusion.44
  547.1 5.0 copy.45
  552.1 15.5 %fusion.16 = bf16[6,64,16,128]{3,1,2,0:T(8,128)(2,1)S(1)} fusion(bf16[6,256,16,128]{3,2,1,0:T(8,128)(2,1)} %bitcast.94, f32[6,16,64]{2,1,0:T(8,128)S(1)} %fusion.44, f32[6,16,256,64]{2,3,1,0:T(8,128)} %copy-done.2), kind=kOutput, calls=%fused_computation.24 | convolution fusion | flops 411310336 | bytes 14180352 | tf_op jit(solution)/shard_map/chqk,ckhd->cqhd/dot_general | solution.py:117
  567.6 1.0 copy.42
  568.6 1.6 copy.58
  (165 shorter events, 3.2 us)
Async XLA Ops:
  7.2 393.3 %copy-start = (bf16[64,768]{1,0:T(8,128)(2,1)S(1)}, bf16[64,768]{1,0:T(8,128)(2,1)}, u32[]{:S(2)}) copy-start(bf16[64,768]{1,0:T(8,128)(2,1)} %param.9) | copy-start | bytes 294916
  43.0 6.3 %copy-start.4 = (bf16[6,768]{1,0:T(8,128)(2,1)S(1)}, bf16[6,768]{1,0:T(8,128)(2,1)}, u32[]{:S(2)}) copy-start(bf16[6,768]{1,0:T(8,128)(2,1)} %param.8) | copy-start | bytes 27652
  43.0 348.7 %copy-start.3 = (bf16[384,2048]{1,0:T(8,128)(2,1)S(1)}, bf16[384,2048]{1,0:T(8,128)(2,1)}, u32[]{:S(2)}) copy-start(bf16[384,2048]{1,0:T(8,128)(2,1)} %param.12) | copy-start | bytes 4718596
  43.0 465.3 %all-to-all-start.1 = ((bf16[64,2,64,896]{3,2,1,0:T(8,128)(2,1)}), bf16[64,2,64,896]{3,2,1,0:T(8,128)(2,1)}, u32[]{:S(2)}, u32[]{:S(2)}) async-start(bf16[64,2,64,896]{3,2,1,0:T(8,128)(2,1)} %bitcast.92), calls=%async_computation.1 | async-start | bytes 29360128 | tf_op jit(solution)/shard_map/all_to_all | solution.py:97
  49.2 465.3 %all-gather.4.cloned.1.call-start = ((), (), s32[]{:S(2)}) async-start(), calls=%async_computation.2 | async-start | bytes 7454720 | tf_op jit(solution)/shard_map/all_gather | solution.py:105
  49.3 1.6 collective-permute-start
  50.9 316.3 %collective-permute-start.1 = (bf16[2,6,768]{2,1,0:T(8,128)(2,1)S(1)}, bf16[2,6,768]{2,1,0:T(8,128)(2,1)S(1)}, u32[]{:S(2)}, u32[]{:S(2)}) collective-permute-start(bf16[2,6,768]{2,1,0:T(8,128)(2,1)S(1)} %get-tuple-element.163), channel_id=1, source_target_pairs={{0,8},{4,12},{8,0},{12,4},{16,24},{20,28},{24,16},{28,20},{32,40},... | collective-permute-start | bytes 55304 | tf_op jit(solution)/shard_map/ppermute | solution.py:25
  367.2 4.5 collective-permute-start.2
  371.7 8.9 %collective-permute-start.3 = (bf16[8,6,768]{2,1,0:T(8,128)(2,1)S(1)}, bf16[8,6,768]{2,1,0:T(8,128)(2,1)S(1)}, u32[]{:S(2)}, u32[]{:S(2)}) collective-permute-start(bf16[8,6,768]{2,1,0:T(8,128)(2,1)S(1)} %bitcast.104), channel_id=1, source_target_pairs={{0,32},{4,36},{8,40},{12,44},{16,48},{20,52},{24,56},{28,60},{32,0... | collective-permute-start | bytes 221192 | tf_op jit(solution)/shard_map/ppermute | solution.py:25
  380.6 8.1 %collective-permute-start.4 = (bf16[16,6,768]{2,1,0:T(8,128)(2,1)S(1)}, bf16[16,6,768]{2,1,0:T(8,128)(2,1)S(1)}, u32[]{:S(2)}, u32[]{:S(2)}) collective-permute-start(bf16[16,6,768]{2,1,0:T(8,128)(2,1)S(1)} %bitcast.102), channel_id=1, source_target_pairs={{0,64},{4,68},{8,72},{12,76},{16,80},{20,84},{24,88},{28,92},{32,9... | collective-permute-start | bytes 442376 | tf_op jit(solution)/shard_map/ppermute | solution.py:25
  388.9 11.0 %collective-permute-start.5 = (bf16[32,6,768]{2,1,0:T(8,128)(2,1)S(1)}, bf16[32,6,768]{2,1,0:T(8,128)(2,1)S(1)}, u32[]{:S(2)}, u32[]{:S(2)}) collective-permute-start(bf16[32,6,768]{2,1,0:T(8,128)(2,1)S(1)} %bitcast.100), channel_id=1, source_target_pairs={{0,128},{4,132},{8,136},{12,140},{16,144},{20,148},{24,152},{28,15... | collective-permute-start | bytes 884744 | tf_op jit(solution)/shard_map/ppermute | solution.py:25
  544.7 7.4 %copy-start.2 = (f32[6,16,256,64]{2,3,1,0:T(8,128)}, f32[6,16,256,64]{2,3,1,0:T(8,128)S(1)}, u32[]{:S(2)}) copy-start(f32[6,16,256,64]{2,3,1,0:T(8,128)S(1)} %fusion.5) | copy-start | bytes 18874372
  552.1 18.1 %copy-start.1 = (bf16[64,768]{1,0:T(8,128)(2,1)S(1)}, bf16[64,768]{1,0:T(8,128)(2,1)}, u32[]{:S(2)}) copy-start(bf16[64,768]{1,0:T(8,128)(2,1)} %param.9) | copy-start | bytes 294916
Sparse Core Ops, SparseCore 0:
  384.4 81.6 all-gather.3
